TPU v7x, 128 devices: a whole 4x4x4 slice. The times are simulated.
128 devices in a mesh: grp: 16 (over x, y), tp: 8 (over z, core).
Axes of the slice: x: 4, y: 4, z: 4, core: 2. Of those that a mesh axis runs over, the one named last changes fastest.
Arguments:
- hidden: bfloat16 [16384, 8192], P('grp'), may hold values from -300 to 300
- norm_gain: bfloat16 [8192], replicated, may hold values from 0.5 to 1.5
- w_query: bfloat16 [8192, 4096], P(None, 'tp'), may hold values from -0.0625 to 0.0625
- b_query: bfloat16 [4096], P('tp'), may hold values from -4 to 4
- w_key: bfloat16 [8192, 1024], P(None, 'tp'), may hold values from -0.0625 to 0.0625
- b_key: bfloat16 [1024], P('tp'), may hold values from -4 to 4
- w_value: bfloat16 [8192, 1024], P(None, 'tp'), may hold values from -0.0625 to 0.0625
- b_value: bfloat16 [1024], P('tp'), may hold values from -4 to 4
- kv_pool: bfloat16 [768, 64, 2048], P('grp', None, 'tp'), may hold values from -100 to 100
- page_table: int32 [256, 3], P('grp'), may hold values from 0 to 47, as said below
- prefix_len: int32 [256], P('grp'), may hold values from 0 to 192, as said below
- request_group: int32 [256, 1], replicated, may hold values from 0 to 15; in each aligned block of 16 rows (0 to 15, 16 to 31, ...) at most 2 rows name the same one
Outputs:
- attn_out: bfloat16 [16384, 4096], P('grp', 'tp')
- decode_pages: bfloat16 [2048, 64, 2048], P('grp', 'tp')
Inputs may be any that keep to these rules, and one draw needn't show every extreme that they name: `request_group`: in the rows of one group (aligned blocks of 16 rows) each decode group is named at most 2 times. `prefix_len`: a multiple of 64. `page_table`: the rows of one group name each of its 48 pool pages once.
All inputs are finite; a program needn't handle non-finite values.
Results may differ from a plain program's by a relative error of at most 0.0076.
Values may be sent and summed in bfloat16 or wider, within the bound.
A program may use at most 192 MiB of HBM per device.

v0:
```python
import math

import jax
import jax.numpy as jnp
from jax import lax
from jax.sharding import PartitionSpec as P

HS = 128
PAGE = 64
PAIR_MOST = 2


rope_base = 1000000.0
norm_eps = 1e-06


def rotate(values, positions):
    half_size = values.shape[-1] // 2
    inverse = rope_base ** (-(jnp.arange(half_size, dtype=jnp.float32) * 2.0) / (2 * half_size))
    angles = positions.astype(jnp.float32)[:, :, None] * inverse[None, None, :]
    cosine = jnp.cos(angles)[:, :, None, :]
    sine_part = jnp.sin(angles)[:, :, None, :]
    first = values[..., :half_size]
    second = values[..., half_size:]
    return jnp.concatenate(
        [first * cosine - second * sine_part, second * cosine + first * sine_part], axis=-1
    )


def rank_within(targets, owners):
    count = targets.shape[0]
    order = jnp.arange(count, dtype=jnp.int32)
    before = (
        (order[None, :] < order[:, None])
        & (owners[None, :] == owners[:, None])
        & (targets[None, :] == targets[:, None])
    )
    return jnp.sum(before.astype(jnp.int32), axis=1)


def local(
    hidden,
    norm_gain,
    w_query,
    b_query,
    w_key,
    b_key,
    w_value,
    b_value,
    kv_pool,
    page_table,
    prefix_len,
    request_group,
):
    group_count = lax.axis_size("grp")
    rank_count = lax.axis_size("tp")
    group_index = lax.axis_index("grp")
    local_requests = prefix_len.shape[0]
    head_size = HS
    kv_heads = w_key.shape[1] // head_size
    query_heads = w_query.shape[1] // head_size
    share_count = query_heads // kv_heads
    kv_cols = 2 * kv_heads * head_size
    page_count = page_table.shape[1] + 1
    page_rows = PAGE // rank_count
    widened = hidden.astype(jnp.float32)
    inv_rms = lax.rsqrt(jnp.mean(widened * widened, axis=1, keepdims=True) + norm_eps)
    normed = (widened * inv_rms * norm_gain.astype(jnp.float32)).astype(jnp.bfloat16)
    query = jnp.dot(normed, w_query, preferred_element_type=jnp.float32) + b_query.astype(
        jnp.float32
    )
    keys_new = jnp.dot(normed, w_key, preferred_element_type=jnp.float32) + b_key.astype(
        jnp.float32
    )
    values_new = jnp.dot(normed, w_value, preferred_element_type=jnp.float32) + b_value.astype(
        jnp.float32
    )
    positions = prefix_len[:, None] + jnp.arange(PAGE, dtype=jnp.int32)[None, :]
    query_rot = rotate(
        query.reshape(local_requests, PAGE, query_heads, head_size), positions
    ).astype(jnp.bfloat16)
    key_rot = rotate(keys_new.reshape(local_requests, PAGE, kv_heads, head_size), positions).astype(
        jnp.bfloat16
    )
    value_store = values_new.reshape(local_requests, PAGE, kv_heads, head_size).astype(jnp.bfloat16)
    new_page = jnp.concatenate([key_rot, value_store], axis=3).reshape(
        local_requests, PAGE, kv_cols
    )
    prefix_pages = prefix_len // PAGE
    page_ids = jnp.arange(page_count, dtype=jnp.int32)[None, :]
    earlier = kv_pool[page_table]
    earlier = jnp.where(
        (page_ids[:, :-1] < prefix_pages[:, None])[:, :, None, None],
        earlier,
        jnp.zeros_like(earlier),
    )
    padded = jnp.concatenate([earlier, jnp.zeros_like(earlier[:, :1])], axis=1)
    request_pages = jnp.where(
        (page_ids == prefix_pages[:, None])[:, :, None, None], new_page[:, None], padded
    )
    targets_all = request_group[:, 0]
    owners_all = jnp.arange(targets_all.shape[0], dtype=jnp.int32) // local_requests
    ranks_all = rank_within(targets_all, owners_all)
    targets_own = lax.dynamic_slice_in_dim(
        targets_all, group_index * local_requests, local_requests
    )
    ranks_own = lax.dynamic_slice_in_dim(ranks_all, group_index * local_requests, local_requests)
    dest_ids = jnp.arange(group_count, dtype=jnp.int32)[:, None, None]
    slot_ids = jnp.arange(PAIR_MOST, dtype=jnp.int32)[None, :, None]
    selector = (
        (targets_own[None, None, :] == dest_ids) & (ranks_own[None, None, :] == slot_ids)
    ).astype(jnp.bfloat16)
    blocked = request_pages.reshape(local_requests, page_count, rank_count, page_rows, kv_cols)
    outgoing = jnp.einsum(
        "dcj,jpurk->ducprk", selector, blocked, preferred_element_type=jnp.float32
    ).astype(jnp.bfloat16)
    outgoing = outgoing.reshape(group_count * rank_count, PAIR_MOST, page_count, page_rows, kv_cols)
    arrived = lax.all_to_all(outgoing, ("grp", "tp"), split_axis=0, concat_axis=0, tiled=True)
    arrived = arrived.reshape(group_count, rank_count, PAIR_MOST, page_count, page_rows, kv_cols)
    pages_out = arrived.transpose(0, 2, 3, 4, 1, 5).reshape(
        group_count * PAIR_MOST * page_count, page_rows, rank_count * kv_cols
    )
    key_length = page_count * PAGE
    flattened_cache = request_pages.reshape(local_requests, key_length, kv_heads, 2 * head_size)
    cache_keys = flattened_cache[..., :head_size]
    cache_values = flattened_cache[..., head_size:]
    grouped = query_rot.reshape(local_requests, PAGE, kv_heads, share_count, head_size)
    scores = jnp.einsum(
        "rqkgd,rskd->rkgqs", grouped, cache_keys, preferred_element_type=jnp.float32
    ) * (1.0 / math.sqrt(head_size))
    visible = jnp.arange(key_length, dtype=jnp.int32)[None, None, :] <= positions[:, :, None]
    scores = jnp.where(visible[:, None, None], scores, -1e30)
    highest = jnp.max(scores, axis=-1, keepdims=True)
    weights = jnp.exp(scores - highest)
    shares = (weights / jnp.sum(weights, axis=-1, keepdims=True)).astype(jnp.bfloat16)
    blended = jnp.einsum(
        "rkgqs,rskd->rqkgd", shares, cache_values, preferred_element_type=jnp.float32
    )
    attn_out = blended.reshape(local_requests * PAGE, query_heads * head_size).astype(jnp.bfloat16)
    return (attn_out, pages_out)


def solution(mesh):
    in_specs = (
        P("grp", None),
        P(),
        P(None, "tp"),
        P("tp"),
        P(None, "tp"),
        P("tp"),
        P(None, "tp"),
        P("tp"),
        P("grp", None, "tp"),
        P("grp", None),
        P("grp"),
        P(),
    )
    out_specs = (P("grp", "tp"), P("grp", "tp", None))
    return jax.shard_map(local, mesh=mesh, in_specs=in_specs, out_specs=out_specs, check_vma=False)
```

profile of v0, /device:TPU:1, one launch (start us, length us, event | category | flops | bytes accessed | tf_op | source)
XLA Modules:
  0.0 126.6 jit_solution(5737718460768586755)
XLA Ops:
  2.9 7.2 %fusion = f32[1024]{0:T(1024)S(1)} fusion(bf16[1024,8192]{1,0:T(8,128)(2,1)} %param.12), kind=kLoop, calls=%fused_computation.3 | loop fusion | flops 25164800 | bytes 16781312 | tf_op jit(solution)/shard_map/reduce_sum | solution.py:67
  10.6 9.8 %fusion.2 = bf16[1024,8192]{1,0:T(8,128)(2,1)S(1)} fusion(bf16[1024,8192]{1,0:T(8,128)(2,1)} %param.12, f32[8192]{0:T(1024)S(1)} %convert_element_type.78, f32[1024]{0:T(1024)S(1)} %add_rsqrt_fusion), kind=kLoop, calls=%fused_computation.5 | loop fusion | flops 33554432 | bytes 33591296 | tf_op jit(solution)/shard_map/convert_element_type | solution.py:68
  20.4 4.8 %convolution_add_fusion.2 = f32[1024,128]{1,0:T(8,128)S(1)} fusion(bf16[1024,8192]{1,0:T(8,128)(2,1)S(1)} %fusion.2, bf16[8192,128]{1,0:T(8,128)(2,1)S(1)} %copy-done, f32[128]{0:T(128)S(1)} %convert_element_type.80), kind=kOutput, calls=%fused_computation.24 | convolution fusion | flops 2147614720 | bytes 19399168 | tf_op jit(solution)/shard_map/dot_general | solution.py:72
  25.2 1.5 %copy-done.2 = bf16[1024,8192]{1,0:T(8,128)(2,1)} copy-done((bf16[1024,8192]{1,0:T(8,128)(2,1)}, bf16[1024,8192]{1,0:T(8,128)(2,1)S(1)}, u32[]{:S(2)}) %copy-start.2) | copy-done | bytes 16777240
  26.7 4.8 %fusion.14 = bf16[1024,128]{1,0:T(8,128)(2,1)S(1)} fusion(bf16[1024,8192]{1,0:T(8,128)(2,1)S(1)} %fusion.2, bf16[8192,128]{1,0:T(8,128)(2,1)S(1)} %copy-done.8, f32[128]{0:T(128)S(1)} %convert_element_type.82), kind=kOutput, calls=%fused_computation.23 | convolution fusion | flops 2147745792 | bytes 19137024 | tf_op jit(solution)/shard_map/dot_general | solution.py:75
  31.5 2.1 %gather_fusion = bf16[48,64,256]{2,1,0:T(8,128)(2,1)S(1)} fusion(bf16[48,64,256]{2,1,0:T(8,128)(2,1)} %param.20, s32[1024]{0:T(1024)S(1)} %pad_clamp_fusion), kind=kCustom, calls=%fused_computation | custom fusion | bytes 3145920 | tf_op jit(solution)/shard_map/gather | solution.py:91
  33.7 2.5 %fusion.24 = (bf16[16,64,1,64]{3,1,0,2:T(8,128)(2,1)S(1)}, bf16[16,64,1,64]{3,1,0,2:T(8,128)(2,1)S(1)}) fusion(f32[16,64,1,128]{3,1,0,2:T(8,128)S(1)} %bitcast.90, f32[64]{0:T(128)S(1)} %multiply_power_fusion, f32[16,64]{1,0:T(8,128)S(1)} %get-tuple-element.11), kind=kLoop, calls=%fused_computation.42 | loop fusion | flops 589824 | bytes 790784 | tf_op jit(solution)/shard_map/convert.2
  36.8 1.3 %copy-done.3 = bf16[16,4,64,256]{3,2,1,0:T(8,128)(2,1)} copy-done((bf16[16,4,64,256]{3,2,1,0:T(8,128)(2,1)}, bf16[16,4,64,256]{3,2,1,0:T(8,128)(2,1)S(1)}, u32[]{:S(2)}) %copy-start.3) | copy-done | bytes 2097176
  38.1 1.2 copy.35
  39.7 1.2 convert_bitcast_fusion
  40.9 4.4 %copy.36 = bf16[16,8,2,4,8,256]{5,4,3,2,1,0:T(8,128)(2,1)} copy(bf16[16,8,2,4,8,256]{5,0,2,4,1,3:T(8,128)(2,1)S(1)} %convert_bitcast_fusion) | data formatting | bytes 8388608 | tf_op jit(solution)/shard_map/convert_element_type | solution.py:116
  45.4 12.0 %all-to-all-start = ((bf16[128,2,4,8,256]{4,3,2,1,0:T(8,128)(2,1)}), bf16[128,2,4,8,256]{4,3,2,1,0:T(8,128)(2,1)}, u32[]{:S(2)}, u32[]{:S(2)}) async-start(bf16[128,2,4,8,256]{4,3,2,1,0:T(8,128)(2,1)} %bitcast.84), calls=%async_computation | async-start | bytes 8388608 | tf_op jit(solution)/shard_map/all_to_all | solution.py:118
  57.3 15.8 %convolution_add_fusion = f32[1024,512]{1,0:T(8,128)} fusion(bf16[1024,8192]{1,0:T(8,128)(2,1)} %copy-done.2, bf16[8192,512]{1,0:T(8,128)(2,1)} %param.14, f32[512]{0:T(512)S(1)} %convert_element_type.85), kind=kOutput, calls=%fused_computation.18 | convolution fusion | flops 8590458880 | bytes 27265024 | tf_op jit(solution)/shard_map/dot_general | solution.py:69
  73.1 1.9 %reshape.304 = f32[16,64,4,128]{3,2,1,0:T(4,128)S(1)} reshape(f32[1024,512]{1,0:T(8,128)} %convolution_add_fusion) | data formatting | bytes 4194304 | tf_op jit(solution)/shard_map/reshape | solution.py:80
  75.3 1.9 %multiply_cosine_fusion = (f32[16,64,64]{2,1,0:T(8,128)S(1)}, f32[16,64,64]{2,1,0:T(8,128)S(1)}) fusion(f32[64]{0:T(128)S(1)} %multiply_power_fusion, f32[16,64]{1,0:T(8,128)S(1)} %get-tuple-element.11), kind=kLoop, calls=%fused_computation.34 | loop fusion | flops 65536 | bytes 528640 | tf_op jit(solution)/shard_map/cos | solution.py:21
  77.1 1.3 %fusion.37 = (f32[16,64,4,64]{3,2,1,0:T(4,128)S(1)}, f32[16,64,4,64]{3,2,1,0:T(4,128)S(1)}) fusion(f32[16,64,4,128]{3,2,1,0:T(4,128)S(1)} %reshape.304), kind=kLoop, calls=%fused_computation.77 | loop fusion | bytes 4194304 | tf_op jit(solution)/shard_map/slice | solution.py:23
  80.0 1.6 %fusion.4 = (f32[16,4,64]{2,1,0:T(4,128)S(1)}, f32[16,256,64,4]{1,2,3,0:T(8,128)S(1)}) fusion(pred[16,64,256]{2,1,0:T(8,128)(4,1)S(1)} %iota_compare_fusion, bf16[16,64,4,64]{3,1,2,0:T(8,128)(2,1)S(1)} %get-tuple-element.3, bf16[16,64,4,64]{3,1,2,0:T(8,128)(2,1)S(1)} %get-tuple-element.2, bf16[16,256,1,256]{3,1,0,2:T(8,128)(2,1)S(1)} %bitcast.86), kind=kOutput, calls=%fused_computation.11 | convolution fusion | flops 273674240 | bytes 7618560 | tf_op jit(solution)/shard_map/rqkgd,rskd->rkgqs/dot_general | solution.py:128
  81.6 1.6 %fusion.3 = f32[16,4,64]{2,1,0:T(4,128)S(1)} fusion(f32[16,256,64,4]{1,2,3,0:T(8,128)S(1)} %get-tuple-element.13, f32[16,4,64]{2,1,0:T(4,128)S(1)} %get-tuple-element.12, pred[16,64,256]{2,1,0:T(8,128)(4,1)S(1)} %iota_compare_fusion), kind=kLoop, calls=%fused_computation.10 | loop fusion | flops 4190208 | bytes 4489216 | tf_op jit(solution)/shard_map/reduce_sum | solution.py:135
  83.2 2.1 %fusion.11 = bf16[16,64,1,4,128]{4,1,3,0,2:T(8,128)(2,1)S(1)} fusion(f32[16,4,64]{2,1,0:T(4,128)S(1)} %fusion.3, f32[16,4,64]{2,1,0:T(4,128)S(1)} %get-tuple-element.12, f32[16,256,64,4]{1,2,3,0:T(8,128)S(1)} %get-tuple-element.13, pred[16,64,256]{2,1,0:T(8,128)(4,1)S(1)} %iota_compare_fusion, bf16[16,256,1,256]{3,1,0,2:T(8,128)(2,1)S(1)} %bitcast.87), kind=kOutput, calls=%fused_computation.21 | convolution fusion | flops 274202624 | bytes 6619136 | tf_op jit(solution)/shard_map/rkgqs,rskd->rqkgd/dot_general | solution.py:136
  85.3 0.9 copy.34
  86.2 1.2 copy.50
  87.3 22.8 %all-to-all-done = bf16[128,2,4,8,256]{4,3,2,1,0:T(8,128)(2,1)} async-done(((bf16[128,2,4,8,256]{4,3,2,1,0:T(8,128)(2,1)}), bf16[128,2,4,8,256]{4,3,2,1,0:T(8,128)(2,1)}, u32[]{:S(2)}, u32[]{:S(2)}) %all-to-all-start) | async-done | bytes 4194336 | tf_op jit(solution)/shard_map/all_to_all | solution.py:118
  110.1 9.0 %copy.37 = bf16[16,2,4,8,8,256]{5,4,3,2,1,0:T(8,128)(2,1)} copy(bf16[16,2,4,8,8,256]{5,3,2,1,4,0:T(8,128)(2,1)} %bitcast.27) | data formatting | bytes 8388608 | tf_op jit(solution)/shard_map/transpose | solution.py:120
  119.1 7.5 %reshape.309 = bf16[128,8,2048]{2,1,0:T(8,128)(2,1)} reshape(bf16[16,2,4,8,8,256]{5,4,3,2,1,0:T(8,128)(2,1)} %copy.37) | data formatting | bytes 8388608 | tf_op jit(solution)/shard_map/reshape | solution.py:120
  (47 shorter events, 5.5 us)
Async XLA Ops:
  0.6 19.8 %copy-start = (bf16[8192,128]{1,0:T(8,128)(2,1)S(1)}, bf16[8192,128]{1,0:T(8,128)(2,1)}, u32[]{:S(2)}) copy-start(bf16[8192,128]{1,0:T(8,128)(2,1)} %param.16) | copy-start | bytes 6291460
  2.9 7.2 %copy-start.9 = (bf16[128]{0:T(256)(128)(2,1)S(1)}, bf16[128]{0:T(256)(128)(2,1)}, u32[]{:S(2)}) copy-start(bf16[128]{0:T(256)(128)(2,1)} %param.17) | copy-start | bytes 772
  2.9 7.3 %copy-start.10 = (bf16[128]{0:T(256)(128)(2,1)S(1)}, bf16[128]{0:T(256)(128)(2,1)}, u32[]{:S(2)}) copy-start(bf16[128]{0:T(256)(128)(2,1)} %param.19) | copy-start | bytes 772
  2.9 7.5 %copy-start.6 = (s32[16,3]{0,1:T(4,128)S(1)}, s32[16,3]{0,1:T(4,128)}, u32[]{:S(2)}) copy-start(s32[16,3]{0,1:T(4,128)} %param.21) | copy-start | bytes 580
  20.4 6.3 %copy-start.2 = (bf16[1024,8192]{1,0:T(8,128)(2,1)}, bf16[1024,8192]{1,0:T(8,128)(2,1)S(1)}, u32[]{:S(2)}) copy-start(bf16[1024,8192]{1,0:T(8,128)(2,1)S(1)} %fusion.2) | copy-start | bytes 50331652
  20.4 6.3 %copy-start.8 = (bf16[8192,128]{1,0:T(8,128)(2,1)S(1)}, bf16[8192,128]{1,0:T(8,128)(2,1)}, u32[]{:S(2)}) copy-start(bf16[8192,128]{1,0:T(8,128)(2,1)} %param.18) | copy-start | bytes 6291460
  36.7 1.3 %copy-start.3 = (bf16[16,4,64,256]{3,2,1,0:T(8,128)(2,1)}, bf16[16,4,64,256]{3,2,1,0:T(8,128)(2,1)S(1)}, u32[]{:S(2)}) copy-start(bf16[16,4,64,256]{3,2,1,0:T(8,128)(2,1)S(1)} %pad_select_fusion) | copy-start | bytes 6291460
  38.1 1.2 copy-start.5
  45.4 12.0 %copy-start.7 = (bf16[512]{0:T(512)(128)(2,1)S(1)}, bf16[512]{0:T(512)(128)(2,1)}, u32[]{:S(2)}) copy-start(bf16[512]{0:T(512)(128)(2,1)} %param.15) | copy-start | bytes 3076
  45.4 64.7 %all-to-all-start = ((bf16[128,2,4,8,256]{4,3,2,1,0:T(8,128)(2,1)}), bf16[128,2,4,8,256]{4,3,2,1,0:T(8,128)(2,1)}, u32[]{:S(2)}, u32[]{:S(2)}) async-start(bf16[128,2,4,8,256]{4,3,2,1,0:T(8,128)(2,1)} %bitcast.84), calls=%async_computation | async-start | bytes 8388608 | tf_op jit(solution)/shard_map/all_to_all | solution.py:118
  78.4 1.6 %copy-start.4 = (bf16[16,4,64,256]{3,2,1,0:T(8,128)(2,1)S(1)}, bf16[16,4,64,256]{3,2,1,0:T(8,128)(2,1)}, u32[]{:S(2)}) copy-start(bf16[16,4,64,256]{3,2,1,0:T(8,128)(2,1)} %copy-done.3) | copy-start | bytes 6291460
  119.1 7.5 %copy-start.1 = (bf16[8192,128]{1,0:T(8,128)(2,1)S(1)}, bf16[8192,128]{1,0:T(8,128)(2,1)}, u32[]{:S(2)}) copy-start(bf16[8192,128]{1,0:T(8,128)(2,1)} %param.16) | copy-start | bytes 6291460
where the time goes:
time: 127 us
  local copies, waits for them, and re-layouts  33.4 us (26%)
  matrix products  30.2 us (24%)
  other arithmetic  27.3 us (21%)
  waiting for transfers between devices  22.8 us (18%)
  starting transfers between devices  12 us (9%)
    all_to_all x1, waiting for transfers between devices, local(): lax.all_to_all(outgoing, ('grp', 'tp'), split_axis=0, concat_axis=0, tile...  22.8 us
    dot_general x1, matrix products, local(): jnp.dot(normed, w_query, preferred_element_type=jnp.float32)  15.8 us
    all_to_all x1, starting transfers between devices, local(): lax.all_to_all(outgoing, ('grp', 'tp'), split_axis=0, concat_axis=0, tile...  12 us
    convert_element_type x1, other arithmetic, local(): (widened * inv_rms * norm_gain.astype(jnp.float32)).astype(jnp.bfloat16)  9.79 us
    transpose x1, local copies, waits for them, and re-layouts, local(): arrived.transpose(0, 2, 3, 4, 1, 5)  8.97 us
    reshape x1, local copies, waits for them, and re-layouts, local(): arrived.transpose(0, 2, 3, 4, 1, 5)  7.51 us
    reduce_sum x1, other arithmetic, local(): jnp.mean(widened * widened, axis=1, keepdims=True) + norm_eps  7.22 us
    dot_general x1, matrix products, local(): jnp.dot(normed, w_key, preferred_element_type=jnp.float32)  4.79 us
  transfers between devices with their start and end apart: 1, of which 1 were waited for; matrix products, arithmetic and copies ran while one was open for 23% of the time, Pallas kernels for 0%

commit v1 on v0

v1 whole, which is shorter than its diff:
```python
import functools
import math

import jax
import jax.numpy as jnp
import numpy as np
from jax import lax
from jax.experimental import pallas as pl
from jax.experimental.pallas import tpu as pltpu
from jax.sharding import PartitionSpec as P

HS = 128
PAGE = 64
PAIR = 2
GX = 4
GY = 4
GRP = 16
TP = 8
PG = 3
ROPE_BASE = 1000000.0
EPS = 1e-06
MESH = pl.DeviceIdType.MESH
RB = 256
KC = 1024


def rope_tables():
    half = HS // 2
    inverse = np.float32(ROPE_BASE) ** (
        -(np.arange(half, dtype=np.float32) * np.float32(2.0)) / np.float32(HS)
    )
    positions = np.arange((PG + 1) * PAGE, dtype=np.float32)
    angles = (positions[:, None] * inverse.astype(np.float32)[None, :]).astype(np.float32)
    cosine = np.cos(angles.astype(np.float64)).astype(np.float32)
    sine = np.sin(angles.astype(np.float64)).astype(np.float32)
    shape = (PG + 1, PAGE, HS)
    return (
        np.concatenate([cosine, cosine], axis=1).reshape(shape),
        np.concatenate([-sine, sine], axis=1).reshape(shape),
    )


def grp_at(g, i):
    x, y = g // GY, lax.rem(g, GY)
    return lax.rem(x + i // GY, GX) * GY + lax.rem(y + lax.rem(i, GY), GY)


def grp_back(g, i):
    x, y = g // GY, lax.rem(g, GY)
    return lax.rem(x + GX - i // GY, GX) * GY + lax.rem(y + GY - lax.rem(i, GY), GY)


def main_kernel(
    hidden,
    gain,
    w_query,
    b_query,
    w_key,
    b_key,
    w_value,
    b_value,
    pool,
    cos_ref,
    sin_ref,
    page_table,
    prefix_len,
    request_group,
    attn,
    cached,
    fresh,
    meta,
    hid,
    wq,
    wkv,
    poolv,
    ss,
    acc,
    newkv,
    qrot,
    attnv,
    send_a,
    recv_a,
    zsend_b,
    zrecv_b,
    zsend_n,
    zrecv_n,
    send_b,
    send_n,
    send_m,
    table,
    load_sem,
    own_sem,
    a_ss,
    a_rs,
    b_ss,
    b_rs,
    n_ss,
    n_rs,
    m_ss,
    m_rs,
    za_ss,
    za_rs,
    zb_ss,
    zb_rs,
    zn_ss,
    zn_rs,
):
    g = lax.axis_index("grp")
    t = lax.axis_index("tp")
    rows, width = hid.shape
    requests = rows // PAGE
    blocks = rows // RB
    steps = width // KC
    per_block = RB // PAGE
    kvw = 2 * HS

    def cols(who):
        return pl.ds(pl.multiple_of(who * kvw, kvw), kvw)

    loads = [
        pltpu.make_async_copy(pool, poolv, load_sem.at[0]),
        pltpu.make_async_copy(w_key, wkv.at[:, 0:HS], load_sem.at[1]),
        pltpu.make_async_copy(w_value, wkv.at[:, HS : 2 * HS], load_sem.at[2]),
    ]
    for b in range(blocks):
        part = pl.ds(b * RB, RB)
        loads.append(pltpu.make_async_copy(hidden.at[part], hid.at[part], load_sem.at[4 + b]))
    loads.append(pltpu.make_async_copy(w_query, wq, load_sem.at[3]))

    barrier = pltpu.get_barrier_semaphore()

    def greet_grp(i, _):
        pl.semaphore_signal(barrier, inc=1, device_id=(grp_at(g, i), t), device_id_type=MESH)
        return 0

    def greet_tp(i, _):
        pl.semaphore_signal(barrier, inc=1, device_id=(g, lax.rem(t + i, TP)), device_id_type=MESH)
        return 0

    lax.fori_loop(1, GRP, greet_grp, 0)
    lax.fori_loop(1, TP, greet_tp, 0)
    for load in loads:
        load.start()

    def find(d, _):
        first = jnp.int32(requests)
        second = jnp.int32(requests)
        for j in range(requests - 1, -1, -1):
            hit = request_group[g * requests + j] == d
            second = jnp.where(hit, first, second)
            first = jnp.where(hit, jnp.int32(j), first)
        table[2 * d] = first
        table[2 * d + 1] = second
        return 0

    lax.fori_loop(0, GRP, find, 0)

    def slot_of(slot):
        j = table[slot]
        used = j < requests
        jc = jnp.minimum(j, requests - 1)
        n = jnp.where(used, prefix_len[jc] // PAGE, 0)
        return used, jc, n

    loads[0].wait()

    def pack_a(slot, _):
        used, jc, n = slot_of(slot)
        page = poolv[page_table[jc * PG]]
        send_a[slot] = jnp.where(n > 0, page, jnp.zeros_like(page))
        return 0

    lax.fori_loop(0, PAIR * GRP, pack_a, 0)

    def pack_zb(j, _):
        for p in range(1, PG):
            zsend_b[(p - 1) * requests + j] = poolv[page_table[j * PG + p]]
        return 0

    lax.fori_loop(0, requests, pack_zb, 0)

    def pack_m(d, _):
        _, _, n0 = slot_of(2 * d)
        _, _, n1 = slot_of(2 * d + 1)
        row = lax.broadcasted_iota(jnp.int32, (8, 128), 0)
        send_m[d] = jnp.where(row == 0, n0, n1)
        return 0

    lax.fori_loop(0, GRP, pack_m, 0)

    pl.semaphore_wait(barrier, GRP - 1 + TP - 1)

    def two(who):
        return pl.ds(PAIR * who, PAIR)

    def copy_a(i, who):
        d = grp_at(g, i)
        return pltpu.make_async_remote_copy(
            src_ref=send_a.at[two(d)], dst_ref=recv_a.at[two(who)],
            send_sem=a_ss.at[i], recv_sem=a_rs.at[i], device_id=(d, t), device_id_type=MESH,
        )

    def copy_b(i, who):
        d = grp_at(g, i)
        return pltpu.make_async_remote_copy(
            src_ref=send_b.at[two(d)], dst_ref=cached.at[two(who), pl.ds(1, PG - 1)],
            send_sem=b_ss.at[i], recv_sem=b_rs.at[i], device_id=(d, t), device_id_type=MESH,
        )

    def copy_n(i, who):
        d = grp_at(g, i)
        return pltpu.make_async_remote_copy(
            src_ref=send_n.at[two(d)], dst_ref=fresh.at[two(who)],
            send_sem=n_ss.at[i], recv_sem=n_rs.at[i], device_id=(d, t), device_id_type=MESH,
        )

    def copy_m(i, who):
        d = grp_at(g, i)
        return pltpu.make_async_remote_copy(
            src_ref=send_m.at[d], dst_ref=meta.at[who],
            send_sem=m_ss.at[i], recv_sem=m_rs.at[i], device_id=(d, t), device_id_type=MESH,
        )

    def copy_za(i, who):
        u = lax.rem(t + i, TP)
        return pltpu.make_async_remote_copy(
            src_ref=recv_a.at[:, u], dst_ref=cached.at[:, 0, :, cols(who)],
            send_sem=za_ss.at[i], recv_sem=za_rs.at[i], device_id=(g, u), device_id_type=MESH,
        )

    def copy_zb(i, who):
        u = lax.rem(t + i, TP)
        return pltpu.make_async_remote_copy(
            src_ref=zsend_b.at[:, u], dst_ref=zrecv_b.at[:, :, cols(who)],
            send_sem=zb_ss.at[i], recv_sem=zb_rs.at[i], device_id=(g, u), device_id_type=MESH,
        )

    def copy_zn(i, who):
        u = lax.rem(t + i, TP)
        return pltpu.make_async_remote_copy(
            src_ref=zsend_n.at[:, u], dst_ref=zrecv_n.at[:, :, cols(who)],
            send_sem=zn_ss.at[i], recv_sem=zn_rs.at[i], device_id=(g, u), device_id_type=MESH,
        )

    def each(count, copy, me, action):
        def step(i, _):
            made = copy(i, me(i))
            getattr(made, action)()
            return 0

        lax.fori_loop(1, count, step, 0)

    def start_grp(copy):
        each(GRP, copy, lambda i: g, "start")

    def start_tp(copy):
        each(TP, copy, lambda i: t, "start")

    def arrived_grp(copy):
        each(GRP, copy, lambda i: grp_back(g, i), "wait_recv")

    def arrived_tp(copy):
        each(TP, copy, lambda i: lax.rem(t + TP - i, TP), "wait_recv")

    def sent_grp(copy):
        each(GRP, copy, lambda i: g, "wait_send")

    def sent_tp(copy):
        each(TP, copy, lambda i: t, "wait_send")

    own_a = pltpu.make_async_copy(send_a.at[two(g)], recv_a.at[two(g)], own_sem.at[0])
    own_zb = pltpu.make_async_copy(zsend_b.at[:, t], zrecv_b.at[:, :, cols(t)], own_sem.at[1])
    own_zn = pltpu.make_async_copy(zsend_n.at[:, t], zrecv_n.at[:, :, cols(t)], own_sem.at[2])
    own_b = pltpu.make_async_copy(
        send_b.at[two(g)], cached.at[two(g), pl.ds(1, PG - 1)], own_sem.at[3]
    )
    own_n = pltpu.make_async_copy(send_n.at[two(g)], fresh.at[two(g)], own_sem.at[4])
    own_m = pltpu.make_async_copy(send_m.at[g], meta.at[g], own_sem.at[5])
    own_za = pltpu.make_async_copy(recv_a.at[:, t], cached.at[:, 0, :, cols(t)], own_sem.at[6])
    attn_copy = pltpu.make_async_copy(attnv, attn, own_sem.at[7])

    start_tp(copy_zb)
    start_grp(copy_a)
    own_zb.start()
    own_a.start()
    start_grp(copy_m)
    own_m.start()

    loads[1].wait()
    loads[2].wait()
    for b in range(blocks):
        loads[3 + b].wait()

    def rotated(values, n):
        return values * cos_ref[n] + pltpu.roll(values, HS // 2, 1) * sin_ref[n]

    def kv_block(b, _):
        part = pl.ds(pl.multiple_of(b * RB, RB), RB)
        ss[part, :] = jnp.zeros((RB, HS), jnp.float32)
        acc[:, 0:kvw] = jnp.zeros((RB, kvw), jnp.float32)

        def step(c, _):
            deep = pl.ds(pl.multiple_of(c * KC, KC), KC)
            x = hid[part, deep]
            xf = x.astype(jnp.float32)
            total = ss[part, :]
            for k in range(KC // HS):
                piece = xf[:, k * HS : (k + 1) * HS]
                total = total + piece * piece
            ss[part, :] = total
            xg = x * gain[:, deep]
            hid[part, deep] = xg
            acc[:, 0:kvw] += jnp.dot(xg, wkv[deep, :], preferred_element_type=jnp.float32)
            return 0

        lax.fori_loop(0, steps, step, 0)
        scale = lax.rsqrt(jnp.sum(ss[part, :], axis=1, keepdims=True) / width + EPS)
        ss[part, :] = jnp.broadcast_to(scale, (RB, HS))
        keys = acc[:, 0:HS] * scale + b_key[...].astype(jnp.float32)
        values = acc[:, HS:kvw] * scale + b_value[...].astype(jnp.float32)
        for r in range(per_block):
            j = b * per_block + r
            n = prefix_len[j] // PAGE
            span = slice(r * PAGE, (r + 1) * PAGE)
            joined = jnp.concatenate([rotated(keys[span], n), values[span]], axis=1)
            newkv[j] = joined.astype(jnp.bfloat16)
            zsend_n[j] = joined.reshape(TP, PAGE // TP, kvw).astype(jnp.bfloat16)
        return 0

    lax.fori_loop(0, blocks, kv_block, 0)
    start_tp(copy_zn)
    own_zn.start()

    arrived_tp(copy_zb)
    own_zb.wait()

    def pack_b(slot, _):
        used, jc, n = slot_of(slot)
        for p in range(1, PG):
            page = zrecv_b[(p - 1) * requests + jc]
            send_b[slot, p - 1] = jnp.where(n > p, page, jnp.zeros_like(page))
        return 0

    lax.fori_loop(0, PAIR * GRP, pack_b, 0)
    start_grp(copy_b)
    own_b.start()

    arrived_grp(copy_a)
    own_a.wait()
    start_tp(copy_za)
    own_za.start()

    loads[3 + blocks].wait()

    def q_block(b, _):
        part = pl.ds(pl.multiple_of(b * RB, RB), RB)
        acc[...] = jnp.zeros(acc.shape, jnp.float32)

        def step(c, _):
            deep = pl.ds(pl.multiple_of(c * KC, KC), KC)
            acc[...] += jnp.dot(hid[part, deep], wq[deep, :], preferred_element_type=jnp.float32)
            return 0

        lax.fori_loop(0, steps, step, 0)
        scale = ss[part, :]
        for h in range(wq.shape[1] // HS):
            lanes = slice(h * HS, (h + 1) * HS)
            one = acc[:, lanes] * scale + b_query[:, lanes].astype(jnp.float32)
            for r in range(per_block):
                j = b * per_block + r
                n = prefix_len[j] // PAGE
                turned = rotated(one[r * PAGE : (r + 1) * PAGE], n)
                qrot[j, h * PAGE : (h + 1) * PAGE, :] = turned.astype(jnp.bfloat16)
        return 0

    lax.fori_loop(0, blocks, q_block, 0)

    arrived_tp(copy_zn)
    own_zn.wait()

    def pack_n(slot, _):
        used, jc, n = slot_of(slot)
        page = zrecv_n[jc]
        send_n[slot] = jnp.where(used, page, jnp.zeros_like(page))
        return 0

    lax.fori_loop(0, PAIR * GRP, pack_n, 0)
    start_grp(copy_n)
    own_n.start()

    heads = wq.shape[1] // HS
    qrows = heads * PAGE
    length = (PG + 1) * PAGE

    def attend(j, _):
        n = prefix_len[j] // PAGE
        pages = [poolv[page_table[j * PG + p]].reshape(PAGE, kvw) for p in range(PG)]
        pages.append(newkv[j])
        kv = jnp.concatenate(pages, axis=0)
        scores = lax.dot_general(
            qrot[j], kv[:, 0:HS], (((1,), (1,)), ((), ())), preferred_element_type=jnp.float32
        ) * (1.0 / math.sqrt(HS))
        column = lax.broadcasted_iota(jnp.int32, (qrows, length), 1)
        token = lax.rem(lax.broadcasted_iota(jnp.int32, (qrows, length), 0), PAGE)
        limit = jnp.where(column < PG * PAGE, n * PAGE, token + (PG * PAGE + 1))
        scores = jnp.where(column < limit, scores, -1e30)
        highest = jnp.max(scores, axis=1, keepdims=True)
        weights = jnp.exp(scores - highest)
        total = jnp.sum(weights, axis=1, keepdims=True)
        out = jnp.dot(weights.astype(jnp.bfloat16), kv[:, HS:kvw], preferred_element_type=jnp.float32)
        out = (out / total).astype(jnp.bfloat16)
        span = pl.ds(pl.multiple_of(j * PAGE, PAGE), PAGE)
        for h in range(heads):
            attnv[span, h * HS : (h + 1) * HS] = out[h * PAGE : (h + 1) * PAGE]
        return 0

    lax.fori_loop(0, requests, attend, 0)
    attn_copy.start()

    arrived_grp(copy_m)
    arrived_tp(copy_za)
    arrived_grp(copy_b)
    arrived_grp(copy_n)
    for own in (own_za, own_b, own_n, own_m, attn_copy):
        own.wait()
    sent_tp(copy_zb)
    sent_grp(copy_a)
    sent_grp(copy_m)
    sent_tp(copy_zn)
    sent_grp(copy_b)
    sent_tp(copy_za)
    sent_grp(copy_n)


def place_kernel(meta, cached, fresh, out):
    slots = fresh.shape[0]
    for slot in range(slots):
        out[slot, 0:PG] = cached[slot]
        out[slot, PG] = jnp.zeros(fresh.shape[1:], out.dtype)
        out[slot, meta[slot // PAIR, slot % PAIR, 0]] = fresh[slot]


def local(
    hidden, norm_gain, w_query, b_query, w_key, b_key, w_value, b_value,
    kv_pool, page_table, prefix_len, request_group,
):
    rows, width = hidden.shape
    qw = w_query.shape[1]
    requests = prefix_len.shape[0]
    npool = kv_pool.shape[0]
    kvw = kv_pool.shape[2]
    page_rows = PAGE // TP
    full = TP * kvw
    slots = PAIR * GRP
    bf = jnp.bfloat16
    cosine, sine = rope_tables()
    any_ = pl.BlockSpec(memory_space=pl.ANY)
    vmem = pl.BlockSpec(memory_space=pltpu.VMEM)
    smem = pl.BlockSpec(memory_space=pltpu.SMEM)
    dma = pltpu.SemaphoreType.DMA
    attn, cached, fresh, meta = pl.pallas_call(
        main_kernel,
        name="span_and_routes",
        out_shape=[
            jax.ShapeDtypeStruct((rows, qw), bf),
            jax.ShapeDtypeStruct((slots, PG, page_rows, full), bf),
            jax.ShapeDtypeStruct((slots, page_rows, full), bf),
            jax.ShapeDtypeStruct((GRP, 8, 128), jnp.int32),
        ],
        in_specs=[any_, vmem, any_, vmem, any_, vmem, any_, vmem, any_, vmem, vmem, smem, smem, smem],
        out_specs=[any_, any_, any_, any_],
        scratch_shapes=[
            pltpu.VMEM((rows, width), bf),
            pltpu.VMEM((width, qw), bf),
            pltpu.VMEM((width, 2 * HS), bf),
            pltpu.VMEM((npool, TP, page_rows, kvw), bf),
            pltpu.VMEM((rows, HS), jnp.float32),
            pltpu.VMEM((RB, qw), jnp.float32),
            pltpu.VMEM((requests, PAGE, kvw), bf),
            pltpu.VMEM((requests, qw // HS * PAGE, HS), bf),
            pltpu.VMEM((rows, qw), bf),
            pltpu.VMEM((slots, TP, page_rows, kvw), bf),
            pltpu.VMEM((slots, TP, page_rows, kvw), bf),
            pltpu.VMEM(((PG - 1) * requests, TP, page_rows, kvw), bf),
            pltpu.VMEM(((PG - 1) * requests, page_rows, full), bf),
            pltpu.VMEM((requests, TP, page_rows, kvw), bf),
            pltpu.VMEM((requests, page_rows, full), bf),
            pltpu.VMEM((slots, PG - 1, page_rows, full), bf),
            pltpu.VMEM((slots, page_rows, full), bf),
            pltpu.VMEM((GRP, 8, 128), jnp.int32),
            pltpu.SMEM((slots,), jnp.int32),
            dma((4 + rows // RB,)),
            dma((8,)),
            dma((GRP,)), dma((GRP,)),
            dma((GRP,)), dma((GRP,)),
            dma((GRP,)), dma((GRP,)),
            dma((GRP,)), dma((GRP,)),
            dma((TP,)), dma((TP,)),
            dma((TP,)), dma((TP,)),
            dma((TP,)), dma((TP,)),
        ],
        cost_estimate=pl.CostEstimate(
            flops=2 * rows * width * (qw + 2 * HS), bytes_accessed=40 << 20, transcendentals=0
        ),
        compiler_params=pltpu.CompilerParams(
            collective_id=0, has_side_effects=True, vmem_limit_bytes=58 << 20
        ),
    )(
        hidden,
        norm_gain.reshape(1, width),
        w_query,
        b_query.reshape(1, qw),
        w_key,
        b_key.reshape(1, HS),
        w_value,
        b_value.reshape(1, HS),
        kv_pool.reshape(npool, TP, page_rows, kvw),
        jnp.asarray(cosine),
        jnp.asarray(sine),
        page_table.reshape(-1),
        prefix_len,
        request_group.reshape(-1),
    )
    steps = 4
    part = slots // steps
    pages = pl.pallas_call(
        place_kernel,
        name="place_new_pages",
        grid=(steps,),
        out_shape=jax.ShapeDtypeStruct((slots, PG + 1, page_rows, full), bf),
        in_specs=[
            pl.BlockSpec((part // PAIR, 8, 128), lambda i: (i, 0, 0), memory_space=pltpu.SMEM),
            pl.BlockSpec((part, PG, page_rows, full), lambda i: (i, 0, 0, 0)),
            pl.BlockSpec((part, page_rows, full), lambda i: (i, 0, 0)),
        ],
        out_specs=pl.BlockSpec((part, PG + 1, page_rows, full), lambda i: (i, 0, 0, 0)),
        compiler_params=pltpu.CompilerParams(vmem_limit_bytes=32 << 20),
    )(meta, cached, fresh)
    return attn, pages.reshape(slots * (PG + 1), page_rows, full)


def solution(mesh):
    in_specs = (
        P("grp", None),
        P(),
        P(None, "tp"),
        P("tp"),
        P(None, "tp"),
        P("tp"),
        P(None, "tp"),
        P("tp"),
        P("grp", None, "tp"),
        P("grp", None),
        P("grp"),
        P(),
    )
    out_specs = (P("grp", "tp"), P("grp", "tp", None))
    return jax.shard_map(local, mesh=mesh, in_specs=in_specs, out_specs=out_specs, check_vma=False)
```

time: 127 us -> 90 us (0.71)
  the two profiles are of different devices: /device:TPU:1 before, /device:TPU:5 now
where the time goes in v1:
time: 90 us; the launch traced here: 89.7 us
  Pallas kernels  80.1 us (89%)
  local copies, waits for them, and re-layouts  8.97 us (10%)
    pallas_call x1, Pallas kernels, local(): pl.pallas_call(main_kernel, name='span_and_routes', out_shape=[jax.ShapeD...  76.4 us
    unnamed x10, local copies, waits for them, and re-layouts  5.68 us
    pallas_call x1, Pallas kernels, local(): pl.pallas_call(place_kernel, name='place_new_pages', grid=(steps,), out_s...  3.71 us

profile of v1, /device:TPU:5, one launch (start us, length us, event | category | flops | bytes accessed | tf_op | source)
XLA Modules:
  0.0 89.7 jit_solution(7134678289717751305)
XLA Ops:
  0.6 1.3 %reshape.29.b_query = bf16[1,512]{1,0:T(2,128)(2,1)} reshape(bf16[512]{0:T(512)(128)(2,1)} %param.17) | data formatting | bytes 2048 | tf_op jit(solution)/shard_map/reshape | solution.py:512
  1.9 0.8 copy.17
  2.6 0.7 reshape.33.page_table
  3.3 1.3 %reshape.28.gain = bf16[1,8192]{1,0:T(2,128)(2,1)} reshape(bf16[8192]{0:T(1024)(128)(2,1)} %param.15) | data formatting | bytes 32768 | tf_op jit(solution)/shard_map/reshape | solution.py:510
  4.7 76.4 %span_and_routes.1 = (bf16[1024,512]{1,0:T(8,128)(2,1)}, bf16[32,3,8,2048]{3,2,1,0:T(8,128)(2,1)}, bf16[32,8,2048]{2,1,0:T(8,128)(2,1)}, s32[16,8,128]{2,1,0:T(8,128)}) custom-call(bf16[1024,8192]{1,0:T(8,128)(2,1)} %hidden.1, bf16[1,8192]{1,0:T(2,128)(2,1)} %reshape.28.gain, bf16[8192,512]{1,0:T(8,128)(2,1)} %w_query.1, bf16[1,512]{1,0:T(2,128)(2,1)} %reshape.29.b_query, ...), custom_call_target="tpu_custom_call" | custom-call | flops 12884901888 | bytes 41943040 | tf_op jit(solution)/shard_map/span_and_routes/pallas_call | solution.py:461
  81.1 0.0 copy-start
  81.1 1.9 %copy-done = bf16[32,3,8,2048]{3,2,1,0:T(8,128)(2,1)S(1)} copy-done((bf16[32,3,8,2048]{3,2,1,0:T(8,128)(2,1)S(1)}, bf16[32,3,8,2048]{3,2,1,0:T(8,128)(2,1)}, u32[]{:S(2)}) %copy-start) | copy-done | bytes 3145752
  83.0 0.0 copy-start.1
  83.0 1.2 %copy-done.1 = bf16[32,8,2048]{2,1,0:T(8,128)(2,1)S(1)} copy-done((bf16[32,8,2048]{2,1,0:T(8,128)(2,1)S(1)}, bf16[32,8,2048]{2,1,0:T(8,128)(2,1)}, u32[]{:S(2)}) %copy-start.1) | copy-done | bytes 1048600
  84.2 0.0 copy-start.2
  84.2 0.8 copy-done.2
  85.0 0.0 copy-start.3
  85.0 3.7 %place_new_pages.1 = bf16[32,4,8,2048]{3,2,1,0:T(8,128)(2,1)} custom-call(s32[16,8,128]{2,1,0:T(8,128)S(1)} %copy-done.2, bf16[32,3,8,2048]{3,2,1,0:T(8,128)(2,1)S(1)} %copy-done, bf16[32,8,2048]{2,1,0:T(8,128)(2,1)S(1)} %copy-done.1), custom_call_target="tpu_custom_call" | custom-call | tf_op jit(solution)/shard_map/place_new_pages/pallas_call | solution.py:526
  88.7 0.0 copy-done.3
  88.7 1.0 %copy.19 = bf16[1024,512]{1,0:T(8,128)(2,1)} copy(bf16[1024,512]{1,0:T(8,128)(2,1)S(1)} %copy-done.3) | data formatting | bytes 2097152
Async XLA Ops:
  81.1 1.9 %copy-start = (bf16[32,3,8,2048]{3,2,1,0:T(8,128)(2,1)S(1)}, bf16[32,3,8,2048]{3,2,1,0:T(8,128)(2,1)}, u32[]{:S(2)}) copy-start(bf16[32,3,8,2048]{3,2,1,0:T(8,128)(2,1)} %get-tuple-element.8.cached) | copy-start | bytes 9437188
  83.0 1.2 %copy-start.1 = (bf16[32,8,2048]{2,1,0:T(8,128)(2,1)S(1)}, bf16[32,8,2048]{2,1,0:T(8,128)(2,1)}, u32[]{:S(2)}) copy-start(bf16[32,8,2048]{2,1,0:T(8,128)(2,1)} %get-tuple-element.9.fresh) | copy-start | bytes 3145732
  84.2 0.8 copy-start.2
  85.0 3.7 %copy-start.3 = (bf16[1024,512]{1,0:T(8,128)(2,1)S(1)}, bf16[1024,512]{1,0:T(8,128)(2,1)}, u32[]{:S(2)}) copy-start(bf16[1024,512]{1,0:T(8,128)(2,1)} %get-tuple-element.12) | copy-start | bytes 3145732

commit v2 on v1

--- a/solution.py
+++ b/solution.py
@@ -40,14 +40,22 @@
     )
 
 
+ORDER = (
+    (2, 2), (0, 1), (1, 0), (2, 1), (1, 2), (0, 3), (3, 0), (2, 3),
+    (3, 2), (1, 1), (3, 3), (0, 2), (2, 0), (1, 3), (3, 1),
+)
+
+
 def grp_at(g, i):
     x, y = g // GY, lax.rem(g, GY)
-    return lax.rem(x + i // GY, GX) * GY + lax.rem(y + lax.rem(i, GY), GY)
+    dx, dy = ORDER[i - 1]
+    return lax.rem(x + dx, GX) * GY + lax.rem(y + dy, GY)
 
 
 def grp_back(g, i):
     x, y = g // GY, lax.rem(g, GY)
-    return lax.rem(x + GX - i // GY, GX) * GY + lax.rem(y + GY - lax.rem(i, GY), GY)
+    dx, dy = ORDER[i - 1]
+    return lax.rem(x + GX - dx, GX) * GY + lax.rem(y + GY - dy, GY)
 
 
 def main_kernel(
@@ -65,10 +73,8 @@
     page_table,
     prefix_len,
     request_group,
-    attn,
-    cached,
-    fresh,
-    meta,
+    attnv,
+    pages,
     hid,
     wq,
     wkv,
@@ -77,7 +83,10 @@
     acc,
     newkv,
     qrot,
-    attnv,
+    fresh,
+    metav,
+    metas,
+    gains,
     send_a,
     recv_a,
     zsend_b,
@@ -129,16 +138,10 @@
 
     barrier = pltpu.get_barrier_semaphore()
 
-    def greet_grp(i, _):
+    for i in range(1, GRP):
         pl.semaphore_signal(barrier, inc=1, device_id=(grp_at(g, i), t), device_id_type=MESH)
-        return 0
-
-    def greet_tp(i, _):
+    for i in range(1, TP):
         pl.semaphore_signal(barrier, inc=1, device_id=(g, lax.rem(t + i, TP)), device_id_type=MESH)
-        return 0
-
-    lax.fori_loop(1, GRP, greet_grp, 0)
-    lax.fori_loop(1, TP, greet_tp, 0)
     for load in loads:
         load.start()
 
@@ -159,34 +162,27 @@
         j = table[slot]
         used = j < requests
         jc = jnp.minimum(j, requests - 1)
-        n = jnp.where(used, prefix_len[jc] // PAGE, 0)
+        n = jnp.where(used, prefix_len[jc] // PAGE, -1)
         return used, jc, n
 
     loads[0].wait()
 
-    def pack_a(slot, _):
-        used, jc, n = slot_of(slot)
-        page = poolv[page_table[jc * PG]]
-        send_a[slot] = jnp.where(n > 0, page, jnp.zeros_like(page))
-        return 0
-
-    lax.fori_loop(0, PAIR * GRP, pack_a, 0)
+    def pack_a(d, _):
+        for k in range(PAIR):
+            slot = PAIR * d + k
+            used, jc, n = slot_of(slot)
+            page = poolv[page_table[0, jc]]
+            send_a[slot] = jnp.where(n > 0, page, jnp.zeros_like(page))
+        return 0
+
+    lax.fori_loop(0, GRP, pack_a, 0)
 
     def pack_zb(j, _):
         for p in range(1, PG):
-            zsend_b[(p - 1) * requests + j] = poolv[page_table[j * PG + p]]
+            zsend_b[(p - 1) * requests + j] = poolv[page_table[p, j]]
         return 0
 
     lax.fori_loop(0, requests, pack_zb, 0)
-
-    def pack_m(d, _):
-        _, _, n0 = slot_of(2 * d)
-        _, _, n1 = slot_of(2 * d + 1)
-        row = lax.broadcasted_iota(jnp.int32, (8, 128), 0)
-        send_m[d] = jnp.where(row == 0, n0, n1)
-        return 0
-
-    lax.fori_loop(0, GRP, pack_m, 0)
 
     pl.semaphore_wait(barrier, GRP - 1 + TP - 1)
 
@@ -203,7 +199,7 @@
     def copy_b(i, who):
         d = grp_at(g, i)
         return pltpu.make_async_remote_copy(
-            src_ref=send_b.at[two(d)], dst_ref=cached.at[two(who), pl.ds(1, PG - 1)],
+            src_ref=send_b.at[two(d)], dst_ref=pages.at[two(who), pl.ds(1, PG - 1)],
             send_sem=b_ss.at[i], recv_sem=b_rs.at[i], device_id=(d, t), device_id_type=MESH,
         )
 
@@ -217,14 +213,14 @@
     def copy_m(i, who):
         d = grp_at(g, i)
         return pltpu.make_async_remote_copy(
-            src_ref=send_m.at[d], dst_ref=meta.at[who],
+            src_ref=send_m.at[d], dst_ref=metav.at[who],
             send_sem=m_ss.at[i], recv_sem=m_rs.at[i], device_id=(d, t), device_id_type=MESH,
         )
 
     def copy_za(i, who):
         u = lax.rem(t + i, TP)
         return pltpu.make_async_remote_copy(
-            src_ref=recv_a.at[:, u], dst_ref=cached.at[:, 0, :, cols(who)],
+            src_ref=recv_a.at[:, u], dst_ref=pages.at[:, 0, :, cols(who)],
             send_sem=za_ss.at[i], recv_sem=za_rs.at[i], device_id=(g, u), device_id_type=MESH,
         )
 
@@ -242,49 +238,59 @@
             send_sem=zn_ss.at[i], recv_sem=zn_rs.at[i], device_id=(g, u), device_id_type=MESH,
         )
 
-    def each(count, copy, me, action):
-        def step(i, _):
-            made = copy(i, me(i))
-            getattr(made, action)()
-            return 0
-
-        lax.fori_loop(1, count, step, 0)
-
     def start_grp(copy):
-        each(GRP, copy, lambda i: g, "start")
+        for i in range(1, GRP):
+            copy(i, g).start()
 
     def start_tp(copy):
-        each(TP, copy, lambda i: t, "start")
+        for i in range(1, TP):
+            copy(i, t).start()
 
     def arrived_grp(copy):
-        each(GRP, copy, lambda i: grp_back(g, i), "wait_recv")
+        for i in range(1, GRP):
+            copy(i, grp_back(g, i)).wait_recv()
 
     def arrived_tp(copy):
-        each(TP, copy, lambda i: lax.rem(t + TP - i, TP), "wait_recv")
+        for i in range(1, TP):
+            copy(i, lax.rem(t + TP - i, TP)).wait_recv()
 
     def sent_grp(copy):
-        each(GRP, copy, lambda i: g, "wait_send")
+        for i in range(1, GRP):
+            copy(i, g).wait_send()
 
     def sent_tp(copy):
-        each(TP, copy, lambda i: t, "wait_send")
+        for i in range(1, TP):
+            copy(i, t).wait_send()
 
     own_a = pltpu.make_async_copy(send_a.at[two(g)], recv_a.at[two(g)], own_sem.at[0])
     own_zb = pltpu.make_async_copy(zsend_b.at[:, t], zrecv_b.at[:, :, cols(t)], own_sem.at[1])
     own_zn = pltpu.make_async_copy(zsend_n.at[:, t], zrecv_n.at[:, :, cols(t)], own_sem.at[2])
     own_b = pltpu.make_async_copy(
-        send_b.at[two(g)], cached.at[two(g), pl.ds(1, PG - 1)], own_sem.at[3]
+        send_b.at[two(g)], pages.at[two(g), pl.ds(1, PG - 1)], own_sem.at[3]
     )
     own_n = pltpu.make_async_copy(send_n.at[two(g)], fresh.at[two(g)], own_sem.at[4])
-    own_m = pltpu.make_async_copy(send_m.at[g], meta.at[g], own_sem.at[5])
-    own_za = pltpu.make_async_copy(recv_a.at[:, t], cached.at[:, 0, :, cols(t)], own_sem.at[6])
-    attn_copy = pltpu.make_async_copy(attnv, attn, own_sem.at[7])
-
+    own_m = pltpu.make_async_copy(send_m.at[g], metav.at[g], own_sem.at[5])
+    own_za = pltpu.make_async_copy(recv_a.at[:, t], pages.at[:, 0, :, cols(t)], own_sem.at[6])
+    meta_copy = pltpu.make_async_copy(metav, metas, own_sem.at[7])
+
+    start_grp(copy_a)
     start_tp(copy_zb)
-    start_grp(copy_a)
+    own_a.start()
     own_zb.start()
-    own_a.start()
+
+    def pack_m(d, _):
+        _, _, n0 = slot_of(PAIR * d)
+        _, _, n1 = slot_of(PAIR * d + 1)
+        row = lax.broadcasted_iota(jnp.int32, (8, 128), 0)
+        send_m[d] = jnp.where(row == 0, n0, n1)
+        return 0
+
+    lax.fori_loop(0, GRP, pack_m, 0)
     start_grp(copy_m)
     own_m.start()
+
+    for k in range(width // HS):
+        gains[:, k * HS : (k + 1) * HS] = jnp.broadcast_to(gain[k : k + 1, :], (16, HS))
 
     loads[1].wait()
     loads[2].wait()
@@ -308,7 +314,7 @@
                 piece = xf[:, k * HS : (k + 1) * HS]
                 total = total + piece * piece
             ss[part, :] = total
-            xg = x * gain[:, deep]
+            xg = x * gains[0:1, deep]
             hid[part, deep] = xg
             acc[:, 0:kvw] += jnp.dot(xg, wkv[deep, :], preferred_element_type=jnp.float32)
             return 0
@@ -334,14 +340,16 @@
     arrived_tp(copy_zb)
     own_zb.wait()
 
-    def pack_b(slot, _):
-        used, jc, n = slot_of(slot)
-        for p in range(1, PG):
-            page = zrecv_b[(p - 1) * requests + jc]
-            send_b[slot, p - 1] = jnp.where(n > p, page, jnp.zeros_like(page))
-        return 0
-
-    lax.fori_loop(0, PAIR * GRP, pack_b, 0)
+    def pack_b(d, _):
+        for k in range(PAIR):
+            slot = PAIR * d + k
+            used, jc, n = slot_of(slot)
+            for p in range(1, PG):
+                page = zrecv_b[(p - 1) * requests + jc]
+                send_b[slot, p - 1] = jnp.where(n > p, page, jnp.zeros_like(page))
+        return 0
+
+    lax.fori_loop(0, GRP, pack_b, 0)
     start_grp(copy_b)
     own_b.start()
 
@@ -365,7 +373,7 @@
         scale = ss[part, :]
         for h in range(wq.shape[1] // HS):
             lanes = slice(h * HS, (h + 1) * HS)
-            one = acc[:, lanes] * scale + b_query[:, lanes].astype(jnp.float32)
+            one = acc[:, lanes] * scale + b_query[h : h + 1, :].astype(jnp.float32)
             for r in range(per_block):
                 j = b * per_block + r
                 n = prefix_len[j] // PAGE
@@ -378,15 +386,21 @@
     arrived_tp(copy_zn)
     own_zn.wait()
 
-    def pack_n(slot, _):
-        used, jc, n = slot_of(slot)
-        page = zrecv_n[jc]
-        send_n[slot] = jnp.where(used, page, jnp.zeros_like(page))
-        return 0
-
-    lax.fori_loop(0, PAIR * GRP, pack_n, 0)
+    def pack_n(d, _):
+        for k in range(PAIR):
+            slot = PAIR * d + k
+            used, jc, n = slot_of(slot)
+            page = zrecv_n[jc]
+            send_n[slot] = jnp.where(used, page, jnp.zeros_like(page))
+        return 0
+
+    lax.fori_loop(0, GRP, pack_n, 0)
     start_grp(copy_n)
     own_n.start()
+
+    arrived_grp(copy_m)
+    own_m.wait()
+    meta_copy.start()
 
     heads = wq.shape[1] // HS
     qrows = heads * PAGE
@@ -394,7 +408,7 @@
 
     def attend(j, _):
         n = prefix_len[j] // PAGE
-        pages = [poolv[page_table[j * PG + p]].reshape(PAGE, kvw) for p in range(PG)]
+        pages = [poolv[page_table[p, j]].reshape(PAGE, kvw) for p in range(PG)]
         pages.append(newkv[j])
         kv = jnp.concatenate(pages, axis=0)
         scores = lax.dot_general(
@@ -415,14 +429,28 @@
         return 0
 
     lax.fori_loop(0, requests, attend, 0)
-    attn_copy.start()
-
-    arrived_grp(copy_m)
+
+    meta_copy.wait()
     arrived_tp(copy_za)
+    own_za.wait()
     arrived_grp(copy_b)
-    arrived_grp(copy_n)
-    for own in (own_za, own_b, own_n, own_m, attn_copy):
-        own.wait()
+    own_b.wait()
+
+    def place(who):
+        for k in range(PAIR):
+            slot = PAIR * who + k
+            n = metas[who, k, 0]
+            page = fresh[slot]
+            for p in range(PG):
+                pages[slot, p] = jnp.where(n == p, page, pages[slot, p])
+            pages[slot, PG] = jnp.where(n == PG, page, jnp.zeros_like(page))
+
+    own_n.wait()
+    place(g)
+    for i in range(1, GRP):
+        who = grp_back(g, i)
+        copy_n(i, who).wait_recv()
+        place(who)
     sent_tp(copy_zb)
     sent_grp(copy_a)
     sent_grp(copy_m)
@@ -430,14 +458,6 @@
     sent_grp(copy_b)
     sent_tp(copy_za)
     sent_grp(copy_n)
-
-
-def place_kernel(meta, cached, fresh, out):
-    slots = fresh.shape[0]
-    for slot in range(slots):
-        out[slot, 0:PG] = cached[slot]
-        out[slot, PG] = jnp.zeros(fresh.shape[1:], out.dtype)
-        out[slot, meta[slot // PAIR, slot % PAIR, 0]] = fresh[slot]
 
 
 def local(
@@ -458,17 +478,15 @@
     vmem = pl.BlockSpec(memory_space=pltpu.VMEM)
     smem = pl.BlockSpec(memory_space=pltpu.SMEM)
     dma = pltpu.SemaphoreType.DMA
-    attn, cached, fresh, meta = pl.pallas_call(
+    attn, pages = pl.pallas_call(
         main_kernel,
         name="span_and_routes",
         out_shape=[
-            jax.ShapeDtypeStruct((rows, qw), bf),
-            jax.ShapeDtypeStruct((slots, PG, page_rows, full), bf),
-            jax.ShapeDtypeStruct((slots, page_rows, full), bf),
-            jax.ShapeDtypeStruct((GRP, 8, 128), jnp.int32),
+            pltpu.VMEM((rows, qw), bf),
+            pltpu.VMEM((slots, PG + 1, page_rows, full), bf),
         ],
         in_specs=[any_, vmem, any_, vmem, any_, vmem, any_, vmem, any_, vmem, vmem, smem, smem, smem],
-        out_specs=[any_, any_, any_, any_],
+        out_specs=[vmem, vmem],
         scratch_shapes=[
             pltpu.VMEM((rows, width), bf),
             pltpu.VMEM((width, qw), bf),
@@ -478,7 +496,10 @@
             pltpu.VMEM((RB, qw), jnp.float32),
             pltpu.VMEM((requests, PAGE, kvw), bf),
             pltpu.VMEM((requests, qw // HS * PAGE, HS), bf),
-            pltpu.VMEM((rows, qw), bf),
+            pltpu.VMEM((slots, page_rows, full), bf),
+            pltpu.VMEM((GRP, 8, 128), jnp.int32),
+            pltpu.SMEM((GRP, 8, 128), jnp.int32),
+            pltpu.VMEM((16, width), bf),
             pltpu.VMEM((slots, TP, page_rows, kvw), bf),
             pltpu.VMEM((slots, TP, page_rows, kvw), bf),
             pltpu.VMEM(((PG - 1) * requests, TP, page_rows, kvw), bf),
@@ -507,9 +528,9 @@
         ),
     )(
         hidden,
-        norm_gain.reshape(1, width),
+        norm_gain.reshape(width // HS, HS),
         w_query,
-        b_query.reshape(1, qw),
+        b_query.reshape(qw // HS, HS),
         w_key,
         b_key.reshape(1, HS),
         w_value,
@@ -517,25 +538,10 @@
         kv_pool.reshape(npool, TP, page_rows, kvw),
         jnp.asarray(cosine),
         jnp.asarray(sine),
-        page_table.reshape(-1),
+        page_table.T,
         prefix_len,
         request_group.reshape(-1),
     )
-    steps = 4
-    part = slots // steps
-    pages = pl.pallas_call(
-        place_kernel,
-        name="place_new_pages",
-        grid=(steps,),
-        out_shape=jax.ShapeDtypeStruct((slots, PG + 1, page_rows, full), bf),
-        in_specs=[
-            pl.BlockSpec((part // PAIR, 8, 128), lambda i: (i, 0, 0), memory_space=pltpu.SMEM),
-            pl.BlockSpec((part, PG, page_rows, full), lambda i: (i, 0, 0, 0)),
-            pl.BlockSpec((part, page_rows, full), lambda i: (i, 0, 0)),
-        ],
-        out_specs=pl.BlockSpec((part, PG + 1, page_rows, full), lambda i: (i, 0, 0, 0)),
-        compiler_params=pltpu.CompilerParams(vmem_limit_bytes=32 << 20),
-    )(meta, cached, fresh)
     return attn, pages.reshape(slots * (PG + 1), page_rows, full)
 
 

time: 90 us -> 70 us (0.78)
  the two profiles are of different devices: /device:TPU:5 before, /device:TPU:1 now
where the time goes in v2:
time: 70 us; the launch traced here: 69.3 us
  Pallas kernels  65.6 us (94%)
  local copies, waits for them, and re-layouts  2.99 us (4%)
    pallas_call x1, Pallas kernels, local(): pl.pallas_call(main_kernel, name='span_and_routes', out_shape=[pltpu.VMEM...  65.6 us
    unnamed x2, local copies, waits for them, and re-layouts  2.99 us

profile of v2, /device:TPU:1, one launch (start us, length us, event | category | flops | bytes accessed | tf_op | source)
XLA Modules:
  0.0 69.3 jit_solution(7671250109067745813)
XLA Ops:
  0.6 65.6 %span_and_routes.1 = (bf16[1024,512]{1,0:T(8,128)(2,1)S(1)}, bf16[32,4,8,2048]{3,2,1,0:T(8,128)(2,1)S(1)}) custom-call(bf16[1024,8192]{1,0:T(8,128)(2,1)} %hidden.1, bf16[64,128]{1,0:T(8,128)(2,1)} %bitcast.10, bf16[8192,512]{1,0:T(8,128)(2,1)} %w_query.1, bf16[4,128]{1,0:T(4,128)(2,1)} %bitcast.12, bf16[8192,128]{1,0:T(8,128)(2,1)} %w_key.1, ...), custom_call_target="tpu_custom_call" | custom-call | flops 12884901888 | bytes 41943040 | tf_op jit(solution)/shard_map/span_and_routes/pallas_call | solution.py:481
  66.3 1.0 %copy.18 = bf16[1024,512]{1,0:T(8,128)(2,1)} copy(bf16[1024,512]{1,0:T(8,128)(2,1)S(1)} %get-tuple-element.6) | data formatting | bytes 2097152
  67.2 2.0 %copy.19 = bf16[128,8,2048]{2,1,0:T(8,128)(2,1)} copy(bf16[128,8,2048]{2,1,0:T(8,128)(2,1)S(1)} %bitcast.8) | data formatting | bytes 8388608

commit v3 on v2

--- a/solution.py
+++ b/solution.py
@@ -22,6 +22,7 @@
 MESH = pl.DeviceIdType.MESH
 RB = 256
 KC = 1024
+EARLY = 2
 
 
 def rope_tables():
@@ -41,38 +42,46 @@
 
 
 ORDER = (
-    (2, 2), (0, 1), (1, 0), (2, 1), (1, 2), (0, 3), (3, 0), (2, 3),
-    (3, 2), (1, 1), (3, 3), (0, 2), (2, 0), (1, 3), (3, 1),
+    (2, 2), (2, 1), (1, 2), (2, 3), (3, 2), (2, 0), (0, 2), (1, 1),
+    (3, 3), (1, 3), (3, 1), (0, 1), (1, 0), (0, 3), (3, 0),
 )
+
+
+def distance(i):
+    dx, dy = ORDER[i - 1]
+    odd = lax.rem(lax.axis_index("tp"), 2)
+    dx = dx + (GX - 2 * dx) * odd if dx else dx
+    dy = dy + (GY - 2 * dy) * odd if dy else dy
+    return dx, dy
 
 
 def grp_at(g, i):
     x, y = g // GY, lax.rem(g, GY)
-    dx, dy = ORDER[i - 1]
+    dx, dy = distance(i)
     return lax.rem(x + dx, GX) * GY + lax.rem(y + dy, GY)
 
 
 def grp_back(g, i):
     x, y = g // GY, lax.rem(g, GY)
-    dx, dy = ORDER[i - 1]
+    dx, dy = distance(i)
     return lax.rem(x + GX - dx, GX) * GY + lax.rem(y + GY - dy, GY)
 
 
 def main_kernel(
     hidden,
-    gain,
+    gain_in,
     w_query,
-    b_query,
+    b_query_in,
     w_key,
-    b_key,
+    b_key_in,
     w_value,
-    b_value,
+    b_value_in,
     pool,
-    cos_ref,
-    sin_ref,
-    page_table,
-    prefix_len,
-    request_group,
+    cos_in,
+    sin_in,
+    page_table_in,
+    prefix_len_in,
+    request_group_in,
     attnv,
     pages,
     hid,
@@ -97,6 +106,16 @@
     send_n,
     send_m,
     table,
+    gain,
+    b_query,
+    b_key,
+    b_value,
+    cos_ref,
+    sin_ref,
+    page_table,
+    prefix_len,
+    request_group,
+    small_sem,
     load_sem,
     own_sem,
     a_ss,
@@ -142,8 +161,25 @@
         pl.semaphore_signal(barrier, inc=1, device_id=(grp_at(g, i), t), device_id_type=MESH)
     for i in range(1, TP):
         pl.semaphore_signal(barrier, inc=1, device_id=(g, lax.rem(t + i, TP)), device_id_type=MESH)
-    for load in loads:
+    small = [
+        pltpu.make_async_copy(source, target, small_sem.at[i])
+        for i, (source, target) in enumerate(
+            (
+                (request_group_in, request_group),
+                (prefix_len_in, prefix_len),
+                (page_table_in, page_table),
+                (gain_in, gain),
+                (b_query_in, b_query),
+                (b_key_in, b_key),
+                (b_value_in, b_value),
+                (cos_in, cos_ref),
+                (sin_in, sin_ref),
+            )
+        )
+    ]
+    for load in small + loads:
         load.start()
+    small[0].wait()
 
     def find(d, _):
         first = jnp.int32(requests)
@@ -165,21 +201,23 @@
         n = jnp.where(used, prefix_len[jc] // PAGE, -1)
         return used, jc, n
 
-    loads[0].wait()
+    for load in (small[1], small[2], loads[0]):
+        load.wait()
 
     def pack_a(d, _):
         for k in range(PAIR):
             slot = PAIR * d + k
             used, jc, n = slot_of(slot)
-            page = poolv[page_table[0, jc]]
-            send_a[slot] = jnp.where(n > 0, page, jnp.zeros_like(page))
+            for p in range(EARLY):
+                page = poolv[page_table[p, jc]]
+                send_a[p, slot] = jnp.where(n > p, page, jnp.zeros_like(page))
         return 0
 
     lax.fori_loop(0, GRP, pack_a, 0)
 
     def pack_zb(j, _):
-        for p in range(1, PG):
-            zsend_b[(p - 1) * requests + j] = poolv[page_table[p, j]]
+        for p in range(EARLY, PG):
+            zsend_b[(p - EARLY) * requests + j] = poolv[page_table[p, j]]
         return 0
 
     lax.fori_loop(0, requests, pack_zb, 0)
@@ -189,17 +227,20 @@
     def two(who):
         return pl.ds(PAIR * who, PAIR)
 
-    def copy_a(i, who):
-        d = grp_at(g, i)
-        return pltpu.make_async_remote_copy(
-            src_ref=send_a.at[two(d)], dst_ref=recv_a.at[two(who)],
-            send_sem=a_ss.at[i], recv_sem=a_rs.at[i], device_id=(d, t), device_id_type=MESH,
-        )
+    def copy_a(p):
+        def made(i, who):
+            d = grp_at(g, i)
+            return pltpu.make_async_remote_copy(
+                src_ref=send_a.at[p, two(d)], dst_ref=recv_a.at[p, two(who)],
+                send_sem=a_ss.at[p, i], recv_sem=a_rs.at[p, i], device_id=(d, t), device_id_type=MESH,
+            )
+
+        return made
 
     def copy_b(i, who):
         d = grp_at(g, i)
         return pltpu.make_async_remote_copy(
-            src_ref=send_b.at[two(d)], dst_ref=pages.at[two(who), pl.ds(1, PG - 1)],
+            src_ref=send_b.at[two(d)], dst_ref=pages.at[two(who), pl.ds(EARLY, PG - EARLY)],
             send_sem=b_ss.at[i], recv_sem=b_rs.at[i], device_id=(d, t), device_id_type=MESH,
         )
 
@@ -217,12 +258,15 @@
             send_sem=m_ss.at[i], recv_sem=m_rs.at[i], device_id=(d, t), device_id_type=MESH,
         )
 
-    def copy_za(i, who):
-        u = lax.rem(t + i, TP)
-        return pltpu.make_async_remote_copy(
-            src_ref=recv_a.at[:, u], dst_ref=pages.at[:, 0, :, cols(who)],
-            send_sem=za_ss.at[i], recv_sem=za_rs.at[i], device_id=(g, u), device_id_type=MESH,
-        )
+    def copy_za(p):
+        def made(i, who):
+            u = lax.rem(t + i, TP)
+            return pltpu.make_async_remote_copy(
+                src_ref=recv_a.at[p, :, u], dst_ref=pages.at[:, p, :, cols(who)],
+                send_sem=za_ss.at[p, i], recv_sem=za_rs.at[p, i], device_id=(g, u), device_id_type=MESH,
+            )
+
+        return made
 
     def copy_zb(i, who):
         u = lax.rem(t + i, TP)
@@ -262,19 +306,24 @@
         for i in range(1, TP):
             copy(i, t).wait_send()
 
-    own_a = pltpu.make_async_copy(send_a.at[two(g)], recv_a.at[two(g)], own_sem.at[0])
+    own_a = pltpu.make_async_copy(send_a.at[:, two(g)], recv_a.at[:, two(g)], own_sem.at[0])
     own_zb = pltpu.make_async_copy(zsend_b.at[:, t], zrecv_b.at[:, :, cols(t)], own_sem.at[1])
     own_zn = pltpu.make_async_copy(zsend_n.at[:, t], zrecv_n.at[:, :, cols(t)], own_sem.at[2])
     own_b = pltpu.make_async_copy(
-        send_b.at[two(g)], pages.at[two(g), pl.ds(1, PG - 1)], own_sem.at[3]
+        send_b.at[two(g)], pages.at[two(g), pl.ds(EARLY, PG - EARLY)], own_sem.at[3]
     )
     own_n = pltpu.make_async_copy(send_n.at[two(g)], fresh.at[two(g)], own_sem.at[4])
     own_m = pltpu.make_async_copy(send_m.at[g], metav.at[g], own_sem.at[5])
-    own_za = pltpu.make_async_copy(recv_a.at[:, t], pages.at[:, 0, :, cols(t)], own_sem.at[6])
+    own_za = [
+        pltpu.make_async_copy(recv_a.at[p, :, t], pages.at[:, p, :, cols(t)], own_sem.at[8 + p])
+        for p in range(EARLY)
+    ]
     meta_copy = pltpu.make_async_copy(metav, metas, own_sem.at[7])
 
-    start_grp(copy_a)
+    start_grp(copy_a(0))
     start_tp(copy_zb)
+    for p in range(1, EARLY):
+        start_grp(copy_a(p))
     own_a.start()
     own_zb.start()
 
@@ -289,6 +338,8 @@
     start_grp(copy_m)
     own_m.start()
 
+    for load in small[3:]:
+        load.wait()
     for k in range(width // HS):
         gains[:, k * HS : (k + 1) * HS] = jnp.broadcast_to(gain[k : k + 1, :], (16, HS))
 
@@ -344,19 +395,23 @@
         for k in range(PAIR):
             slot = PAIR * d + k
             used, jc, n = slot_of(slot)
-            for p in range(1, PG):
-                page = zrecv_b[(p - 1) * requests + jc]
-                send_b[slot, p - 1] = jnp.where(n > p, page, jnp.zeros_like(page))
+            for p in range(EARLY, PG):
+                page = zrecv_b[(p - EARLY) * requests + jc]
+                send_b[slot, p - EARLY] = jnp.where(n > p, page, jnp.zeros_like(page))
         return 0
 
     lax.fori_loop(0, GRP, pack_b, 0)
     start_grp(copy_b)
     own_b.start()
 
-    arrived_grp(copy_a)
-    own_a.wait()
-    start_tp(copy_za)
-    own_za.start()
+    def pass_on(p):
+        arrived_grp(copy_a(p))
+        if p == 0:
+            own_a.wait()
+        start_tp(copy_za(p))
+        own_za[p].start()
+
+    pass_on(0)
 
     loads[3 + blocks].wait()
 
@@ -381,7 +436,7 @@
                 qrot[j, h * PAGE : (h + 1) * PAGE, :] = turned.astype(jnp.bfloat16)
         return 0
 
-    lax.fori_loop(0, blocks, q_block, 0)
+    lax.fori_loop(0, blocks // 2, q_block, 0)
 
     arrived_tp(copy_zn)
     own_zn.wait()
@@ -397,6 +452,10 @@
     lax.fori_loop(0, GRP, pack_n, 0)
     start_grp(copy_n)
     own_n.start()
+
+    for p in range(1, EARLY):
+        pass_on(p)
+    lax.fori_loop(blocks // 2, blocks, q_block, 0)
 
     arrived_grp(copy_m)
     own_m.wait()
@@ -431,8 +490,9 @@
     lax.fori_loop(0, requests, attend, 0)
 
     meta_copy.wait()
-    arrived_tp(copy_za)
-    own_za.wait()
+    for p in range(EARLY):
+        arrived_tp(copy_za(p))
+        own_za[p].wait()
     arrived_grp(copy_b)
     own_b.wait()
 
@@ -452,12 +512,30 @@
         copy_n(i, who).wait_recv()
         place(who)
     sent_tp(copy_zb)
-    sent_grp(copy_a)
+    for p in range(EARLY):
+        sent_grp(copy_a(p))
+        sent_tp(copy_za(p))
     sent_grp(copy_m)
     sent_tp(copy_zn)
     sent_grp(copy_b)
-    sent_tp(copy_za)
     sent_grp(copy_n)
+
+
+def out_kernel(attnv, pagesv, attn, pages, sems):
+    rows, slots = attnv.shape[0], pagesv.shape[0]
+    copies = []
+    for i in range(slots // 4):
+        part = pl.ds(i * 4, 4)
+        copies.append(pltpu.make_async_copy(pagesv.at[part], pages.at[part], sems.at[i]))
+    for i in range(2):
+        part = pl.ds(i * (rows // 2), rows // 2)
+        copies.append(
+            pltpu.make_async_copy(attnv.at[part], attn.at[part], sems.at[slots // 4 + i])
+        )
+    for copy in copies:
+        copy.start()
+    for copy in copies:
+        copy.wait()
 
 
 def local(
@@ -476,7 +554,6 @@
     cosine, sine = rope_tables()
     any_ = pl.BlockSpec(memory_space=pl.ANY)
     vmem = pl.BlockSpec(memory_space=pltpu.VMEM)
-    smem = pl.BlockSpec(memory_space=pltpu.SMEM)
     dma = pltpu.SemaphoreType.DMA
     attn, pages = pl.pallas_call(
         main_kernel,
@@ -485,7 +562,7 @@
             pltpu.VMEM((rows, qw), bf),
             pltpu.VMEM((slots, PG + 1, page_rows, full), bf),
         ],
-        in_specs=[any_, vmem, any_, vmem, any_, vmem, any_, vmem, any_, vmem, vmem, smem, smem, smem],
+        in_specs=[any_] * 14,
         out_specs=[vmem, vmem],
         scratch_shapes=[
             pltpu.VMEM((rows, width), bf),
@@ -500,23 +577,33 @@
             pltpu.VMEM((GRP, 8, 128), jnp.int32),
             pltpu.SMEM((GRP, 8, 128), jnp.int32),
             pltpu.VMEM((16, width), bf),
-            pltpu.VMEM((slots, TP, page_rows, kvw), bf),
-            pltpu.VMEM((slots, TP, page_rows, kvw), bf),
-            pltpu.VMEM(((PG - 1) * requests, TP, page_rows, kvw), bf),
-            pltpu.VMEM(((PG - 1) * requests, page_rows, full), bf),
+            pltpu.VMEM((EARLY, slots, TP, page_rows, kvw), bf),
+            pltpu.VMEM((EARLY, slots, TP, page_rows, kvw), bf),
+            pltpu.VMEM(((PG - EARLY) * requests, TP, page_rows, kvw), bf),
+            pltpu.VMEM(((PG - EARLY) * requests, page_rows, full), bf),
             pltpu.VMEM((requests, TP, page_rows, kvw), bf),
             pltpu.VMEM((requests, page_rows, full), bf),
-            pltpu.VMEM((slots, PG - 1, page_rows, full), bf),
+            pltpu.VMEM((slots, PG - EARLY, page_rows, full), bf),
             pltpu.VMEM((slots, page_rows, full), bf),
             pltpu.VMEM((GRP, 8, 128), jnp.int32),
             pltpu.SMEM((slots,), jnp.int32),
+            pltpu.VMEM((width // HS, HS), bf),
+            pltpu.VMEM((qw // HS, HS), bf),
+            pltpu.VMEM((1, HS), bf),
+            pltpu.VMEM((1, HS), bf),
+            pltpu.VMEM(cosine.shape, jnp.float32),
+            pltpu.VMEM(sine.shape, jnp.float32),
+            pltpu.SMEM((PG, requests), jnp.int32),
+            pltpu.SMEM((requests,), jnp.int32),
+            pltpu.SMEM((request_group.shape[0],), jnp.int32),
+            dma((9,)),
             dma((4 + rows // RB,)),
-            dma((8,)),
+            dma((8 + EARLY,)),
+            dma((EARLY, GRP)), dma((EARLY, GRP)),
             dma((GRP,)), dma((GRP,)),
             dma((GRP,)), dma((GRP,)),
             dma((GRP,)), dma((GRP,)),
-            dma((GRP,)), dma((GRP,)),
-            dma((TP,)), dma((TP,)),
+            dma((EARLY, TP)), dma((EARLY, TP)),
             dma((TP,)), dma((TP,)),
             dma((TP,)), dma((TP,)),
         ],
@@ -542,6 +629,18 @@
         prefix_len,
         request_group.reshape(-1),
     )
+    attn, pages = pl.pallas_call(
+        out_kernel,
+        name="write_out",
+        out_shape=[
+            jax.ShapeDtypeStruct(attn.shape, bf),
+            jax.ShapeDtypeStruct(pages.shape, bf),
+        ],
+        in_specs=[vmem, vmem],
+        out_specs=[any_, any_],
+        scratch_shapes=[dma((2 + slots // 4,))],
+        compiler_params=pltpu.CompilerParams(vmem_limit_bytes=1 << 20),
+    )(attn, pages)
     return attn, pages.reshape(slots * (PG + 1), page_rows, full)
 
 

time: 70 us -> 60.3 us (0.86)
  Pallas kernels: 65.6 us -> 59.5 us
  local copies, waits for them, and re-layouts: 2.99 us -> 0 us
    pallas_call x1, Pallas kernels: 65.6 us -> 57.1 us  [local(): pl.pallas_call(main_kernel, name='span_and_routes', out_shape=[pltpu.VMEM...]
    unnamed x2 -> x0, local copies, waits for them, and re-layouts: 2.99 us -> none
    pallas_call x0 -> x1, Pallas kernels: none -> 2.42 us  [local(): pl.pallas_call(out_kernel, name='write_out', out_shape=[jax.ShapeDtypeStr...]
where the time goes in v3:
time: 60.3 us; the launch traced here: 60.1 us
  Pallas kernels  59.5 us (99%)
  between operations  0.64 us (1%)
    pallas_call x1, Pallas kernels, local(): pl.pallas_call(main_kernel, name='span_and_routes', out_shape=[pltpu.VMEM...  57.1 us
    pallas_call x1, Pallas kernels, local(): pl.pallas_call(out_kernel, name='write_out', out_shape=[jax.ShapeDtypeStr...  2.42 us

profile of v3, /device:TPU:1, one launch (start us, length us, event | category | flops | bytes accessed | tf_op | source)
XLA Modules:
  0.0 60.1 jit_solution(12317837966567382153)
XLA Ops:
  0.6 57.1 %span_and_routes.1 = (bf16[1024,512]{1,0:T(8,128)(2,1)S(1)}, bf16[32,4,8,2048]{3,2,1,0:T(8,128)(2,1)S(1)}) custom-call(bf16[1024,8192]{1,0:T(8,128)(2,1)} %hidden.1, bf16[64,128]{1,0:T(8,128)(2,1)} %bitcast.10, bf16[8192,512]{1,0:T(8,128)(2,1)} %w_query.1, bf16[4,128]{1,0:T(4,128)(2,1)} %bitcast.12, bf16[8192,128]{1,0:T(8,128)(2,1)} %w_key.1, ...), custom_call_target="tpu_custom_call" | custom-call | flops 12884901888 | bytes 41943040 | tf_op jit(solution)/shard_map/span_and_routes/pallas_call | solution.py:558
  57.7 2.4 %write_out.1 = (bf16[1024,512]{1,0:T(8,128)(2,1)}, bf16[32,4,8,2048]{3,2,1,0:T(8,128)(2,1)}) custom-call(bf16[1024,512]{1,0:T(8,128)(2,1)S(1)} %get-tuple-element.6.attnv, bf16[32,4,8,2048]{3,2,1,0:T(8,128)(2,1)S(1)} %get-tuple-element.7.pagesv), custom_call_target="tpu_custom_call" | custom-call | tf_op jit(solution)/shard_map/write_out/pallas_call | solution.py:632

commit v4 on v3

--- a/solution.py
+++ b/solution.py
@@ -43,7 +43,7 @@
 
 ORDER = (
     (2, 2), (2, 1), (1, 2), (2, 3), (3, 2), (2, 0), (0, 2), (1, 1),
-    (3, 3), (1, 3), (3, 1), (0, 1), (1, 0), (0, 3), (3, 0),
+    (3, 3), (1, 3), (3, 1), (0, 1), (3, 0), (0, 3), (1, 0),
 )
 
 
@@ -505,12 +505,6 @@
                 pages[slot, p] = jnp.where(n == p, page, pages[slot, p])
             pages[slot, PG] = jnp.where(n == PG, page, jnp.zeros_like(page))
 
-    own_n.wait()
-    place(g)
-    for i in range(1, GRP):
-        who = grp_back(g, i)
-        copy_n(i, who).wait_recv()
-        place(who)
     sent_tp(copy_zb)
     for p in range(EARLY):
         sent_grp(copy_a(p))
@@ -518,6 +512,12 @@
     sent_grp(copy_m)
     sent_tp(copy_zn)
     sent_grp(copy_b)
+    own_n.wait()
+    place(g)
+    for i in range(1, GRP):
+        who = grp_back(g, i)
+        copy_n(i, who).wait_recv()
+        place(who)
     sent_grp(copy_n)
 
 

time: 60.3 us -> 60.2 us (level)
  no operation moved by 1% of the time
where the time goes in v4:
time: 60.2 us; the launch traced here: 60.1 us
  Pallas kernels  59.4 us (99%)
  between operations  0.64 us (1%)
    pallas_call x1, Pallas kernels, local(): pl.pallas_call(main_kernel, name='span_and_routes', out_shape=[pltpu.VMEM...  57 us
    pallas_call x1, Pallas kernels, local(): pl.pallas_call(out_kernel, name='write_out', out_shape=[jax.ShapeDtypeStr...  2.42 us

profile of v4, /device:TPU:1, one launch (start us, length us, event | category | flops | bytes accessed | tf_op | source)
XLA Modules:
  0.0 60.1 jit_solution(10181707603561032994)
XLA Ops:
  0.6 57.0 %span_and_routes.1 = (bf16[1024,512]{1,0:T(8,128)(2,1)S(1)}, bf16[32,4,8,2048]{3,2,1,0:T(8,128)(2,1)S(1)}) custom-call(bf16[1024,8192]{1,0:T(8,128)(2,1)} %hidden.1, bf16[64,128]{1,0:T(8,128)(2,1)} %bitcast.10, bf16[8192,512]{1,0:T(8,128)(2,1)} %w_query.1, bf16[4,128]{1,0:T(4,128)(2,1)} %bitcast.12, bf16[8192,128]{1,0:T(8,128)(2,1)} %w_key.1, ...), custom_call_target="tpu_custom_call" | custom-call | flops 12884901888 | bytes 41943040 | tf_op jit(solution)/shard_map/span_and_routes/pallas_call | solution.py:558
  57.6 2.4 %write_out.1 = (bf16[1024,512]{1,0:T(8,128)(2,1)}, bf16[32,4,8,2048]{3,2,1,0:T(8,128)(2,1)}) custom-call(bf16[1024,512]{1,0:T(8,128)(2,1)S(1)} %get-tuple-element.6.attnv, bf16[32,4,8,2048]{3,2,1,0:T(8,128)(2,1)S(1)} %get-tuple-element.7.pagesv), custom_call_target="tpu_custom_call" | custom-call | tf_op jit(solution)/shard_map/write_out/pallas_call | solution.py:632

commit v5 on v4

--- a/solution.py
+++ b/solution.py
@@ -286,6 +286,12 @@
         for i in range(1, GRP):
             copy(i, g).start()
 
+    def start_from(copy, first):
+        for i in range(first, GRP):
+            copy(i, g).start()
+        for i in range(1, first):
+            copy(i, g).start()
+
     def start_tp(copy):
         for i in range(1, TP):
             copy(i, t).start()
@@ -323,7 +329,7 @@
     start_grp(copy_a(0))
     start_tp(copy_zb)
     for p in range(1, EARLY):
-        start_grp(copy_a(p))
+        start_from(copy_a(p), 8)
     own_a.start()
     own_zb.start()
 

time: 60.2 us -> 60.2 us (level)
  no operation moved by 1% of the time
where the time goes in v5:
time: 60.2 us; the launch traced here: 60.1 us
  Pallas kernels  59.4 us (99%)
  between operations  0.64 us (1%)
    pallas_call x1, Pallas kernels, local(): pl.pallas_call(main_kernel, name='span_and_routes', out_shape=[pltpu.VMEM...  57 us
    pallas_call x1, Pallas kernels, local(): pl.pallas_call(out_kernel, name='write_out', out_shape=[jax.ShapeDtypeStr...  2.42 us

profile of v5, /device:TPU:1, one launch (start us, length us, event | category | flops | bytes accessed | tf_op | source)
XLA Modules:
  0.0 60.1 jit_solution(2292724686247272079)
XLA Ops:
  0.6 57.0 %span_and_routes.1 = (bf16[1024,512]{1,0:T(8,128)(2,1)S(1)}, bf16[32,4,8,2048]{3,2,1,0:T(8,128)(2,1)S(1)}) custom-call(bf16[1024,8192]{1,0:T(8,128)(2,1)} %hidden.1, bf16[64,128]{1,0:T(8,128)(2,1)} %bitcast.10, bf16[8192,512]{1,0:T(8,128)(2,1)} %w_query.1, bf16[4,128]{1,0:T(4,128)(2,1)} %bitcast.12, bf16[8192,128]{1,0:T(8,128)(2,1)} %w_key.1, ...), custom_call_target="tpu_custom_call" | custom-call | flops 12884901888 | bytes 41943040 | tf_op jit(solution)/shard_map/span_and_routes/pallas_call | solution.py:564
  57.6 2.4 %write_out.1 = (bf16[1024,512]{1,0:T(8,128)(2,1)}, bf16[32,4,8,2048]{3,2,1,0:T(8,128)(2,1)}) custom-call(bf16[1024,512]{1,0:T(8,128)(2,1)S(1)} %get-tuple-element.6.attnv, bf16[32,4,8,2048]{3,2,1,0:T(8,128)(2,1)S(1)} %get-tuple-element.7.pagesv), custom_call_target="tpu_custom_call" | custom-call | tf_op jit(solution)/shard_map/write_out/pallas_call | solution.py:638
